TPU v7x, 256 devices: a whole 4x4x8 slice. The times are simulated.
256 devices in a mesh: pair: 32 (over x, y, core), virt: 8 (over z).
Axes of the slice: x: 4, y: 4, z: 8, core: 2. Of those that a mesh axis runs over, the one named last changes fastest.
Arguments:
- amps: float32 [8, 2048, 2048], P(None, 'pair', 'virt'), may hold values from -6 to 6
- ints: float32 [8, 2048, 2048], P(None, 'pair', 'virt'), may hold values from -0.125 to 0.125
- panel_of: int32 [32], replicated, may hold values from 0 to 31, each once
- e_occ: float32 [8], replicated, may hold values from -2 to -0.5
- e_vir: float32 [2048], replicated, may hold values from 0.2 to 3
Outputs:
- cycle_update: float32 [8, 8, 2048, 2048], P('virt', None, 'pair')
Inputs may be any that keep to these rules, and one draw needn't show every extreme that they name: panel_of holds each of 0 to 31 once.
All inputs are finite; a program needn't handle non-finite values.
Results may differ from a plain program's by a relative error of at most 0.00007.
Values sent between devices are 32-bit elements; how exact they have to be, the bound alone decides.
No kernel may reach another device: no remote copies, remote signals or barrier semaphores. Data moves between devices by JAX's collectives and lax.ppermute only.
A program may use at most 192 MiB of HBM per device.

v0:
```python
import jax
import jax.numpy as jnp
from jax import lax
from jax.sharding import PartitionSpec as P


def panel_table(panel_of):
    count = panel_of.shape[0]
    targets = jnp.arange(count, dtype=jnp.int32)
    return (panel_of[:, None] == targets[None, :]).astype(jnp.float32)


def body(amps, ints, panel_of, e_occ, e_vir):
    panel = amps.shape[1]
    occ_all = amps.shape[0]
    n_virt = lax.axis_size("virt")
    n_pair = lax.axis_size("pair")
    occ_dev = occ_all // n_virt
    virtuals = e_vir.shape[0]
    placing = panel_table(panel_of)
    my_occ = lax.axis_index("virt") * occ_dev + jnp.arange(occ_dev, dtype=jnp.int32)
    b_rows = lax.axis_index("pair") * panel + jnp.arange(panel, dtype=jnp.int32)
    e_b = e_vir[b_rows]
    denom = (
        e_occ[my_occ][:, None, None, None]
        + e_occ[None, :, None, None]
        - e_b[None, None, :, None]
        - e_vir[None, None, None, :]
    )
    own_rows = lax.all_to_all(amps, "virt", split_axis=0, concat_axis=2, tiled=True)
    int_full = lax.all_gather(ints, "virt", axis=2, tiled=True)
    product = jnp.einsum(
        "xac,jbc->xjba",
        lax.all_gather(own_rows, "pair", axis=1, tiled=True),
        int_full,
        precision=lax.Precision.HIGHEST,
        preferred_element_type=jnp.float32,
    )
    grouped = product.reshape(occ_dev, occ_all, panel, n_pair, panel)
    direct = jnp.einsum(
        "xjbqp,qn->xjbnp",
        grouped,
        placing,
        precision=lax.Precision.HIGHEST,
        preferred_element_type=jnp.float32,
    ).reshape(occ_dev, occ_all, panel, virtuals)
    mirrored = lax.all_to_all(direct, "virt", split_axis=1, concat_axis=1, tiled=True)
    return (direct - mirrored) / denom


def solution(mesh):
    in_specs = (P(None, "pair", "virt"), P(None, "pair", "virt"), P(), P(), P())
    out_specs = P("virt", None, "pair", None)
    return jax.shard_map(body, mesh=mesh, in_specs=in_specs, out_specs=out_specs, check_vma=False)
```

profile of v0, /device:TPU:1, one launch (start us, length us, event | category | flops | bytes accessed | tf_op | source)
XLA Modules:
  0.0 342.6 jit_solution(10947563948808677150)
XLA Ops:
  6.5 0.0 all-gather.3.cloned.1.call-start
  6.5 0.7 all-gather.3.cloned.1.call-update
  7.3 0.0 all-gather.5.cloned.1.call-start
  7.3 26.2 %all_to_all.23 = f32[8,64,256]{2,1,0:T(8,128)S(1)} all-to-all(f32[8,64,256]{2,1,0:T(8,128)} %param.5), channel_id=1, replica_groups=mesh['pair'=32,'virt'=8] {'virt'}, dimensions={0} | all-to-all | bytes 1048576 | tf_op jit(solution)/shard_map/all_to_all | solution.py:30
  33.5 0.8 copy.14
  34.3 0.0 all-gather.5.cloned.1.call-update
  34.4 37.2 %all-gather.3.cloned.1.call-done = f32[8,64,2048]{2,1,0:T(8,128)} async-done(((f32[8,64,256]{2,1,0:T(8,128)}), f32[8,64,2048]{2,1,0:T(8,128)}) %all-gather.3.cloned.1.call-update) | async-done | bytes 4194320 | tf_op jit(solution)/shard_map/all_gather | solution.py:31
  71.6 79.3 %all-gather.5.cloned.1.call-done = f32[1,2048,2048]{2,1,0:T(8,128)} async-done(((f32[1,64,2048]{2,1,0:T(8,128)}), f32[1,2048,2048]{2,1,0:T(8,128)}) %all-gather.5.cloned.1.call-update) | async-done | bytes 16777232 | tf_op jit(solution)/shard_map/all_gather | solution.py:34
  150.9 0.0 copy-start.1
  150.9 57.1 %fusion.2 = f32[8,64,32,64]{3,1,2,0:T(8,128)S(1)} fusion(f32[32,64,2048,1]{2,1,0,3:T(8,128)} %bitcast.38, f32[8,64,2048]{2,1,0:T(8,128)} %all-gather.3.cloned.1.call-done), kind=kOutput, calls=%fused_computation.3 | convolution fusion | flops 25769803776 | bytes 25165824 | tf_op jit(solution)/shard_map/xac,jbc->xjba/dot_general | solution.py:32
  208.0 0.0 copy-done.1
  208.0 10.1 %fusion.4 = f32[1,8,64,32,64]{4,3,2,1,0:T(8,128)} fusion(f32[8,64,32,64]{3,1,2,0:T(8,128)S(1)} %fusion.2, s32[32]{0:T(128)S(1)} %copy-done.1), kind=kOutput, calls=%fused_computation.6 | convolution fusion | flops 402654208 | bytes 8388736 | tf_op jit(solution)/shard_map/xjbqp,qn->xjbnp/dot_general | solution.py:40
  218.1 7.8 %reshape.79 = f32[1,8,64,2048]{3,2,1,0:T(8,128)} reshape(f32[1,8,64,32,64]{4,3,2,1,0:T(8,128)} %fusion.4) | data formatting | bytes 8388608 | tf_op jit(solution)/shard_map/reshape | solution.py:46
  225.9 0.0 copy-start
  225.9 0.0 copy-start.2
  225.9 6.9 %all-to-all-start.1 = ((f32[1,8,64,2048]{3,2,0,1:T(8,128)}), f32[1,8,64,2048]{3,2,0,1:T(8,128)}, u32[]{:S(2)}, u32[]{:S(2)}) async-start(f32[1,8,64,2048]{3,2,0,1:T(8,128)} %bitcast.35), calls=%async_computation.1 | async-start | bytes 8388608 | tf_op jit(solution)/shard_map/all_to_all | solution.py:47
  232.8 0.0 copy-done
  232.8 0.8 gather_fusion
  233.6 0.0 copy-done.2
  233.6 0.6 dynamic-slice.2
  234.2 0.6 broadcast_add_fusion
  234.8 0.1 broadcast_subtract_fusion
  234.8 94.8 %all-to-all-done.1 = f32[1,8,64,2048]{3,2,0,1:T(8,128)} async-done(((f32[1,8,64,2048]{3,2,0,1:T(8,128)}), f32[1,8,64,2048]{3,2,0,1:T(8,128)}, u32[]{:S(2)}, u32[]{:S(2)}) %all-to-all-start.1) | async-done | bytes 4194336 | tf_op jit(solution)/shard_map/all_to_all | solution.py:47
  329.6 6.1 %divide_bitcast_fusion = f32[1,8,64,2048]{3,2,1,0:T(8,128)} fusion(f32[1,8,64,2048]{3,2,0,1:T(8,128)} %all-to-all-done.1, f32[2048]{0:T(1024)S(1)} %copy-done, f32[8,64]{1,0:T(8,128)S(1)} %broadcast_subtract_fusion, f32[1,8,64,2048]{3,2,1,0:T(8,128)} %reshape.79), kind=kLoop, calls=%fused_computation.5 | loop fusion | flops 3145728 | bytes 12593152 | tf_op jit(solution)/shard_map/div | solution.py:48
  (2 shorter events, 0.0 us)
Async XLA Ops:
  6.5 65.0 %all-gather.3.cloned.1.call-start = ((), (), s32[]{:S(2)}) async-start(), calls=%async_computation.2 | async-start | bytes 4718592 | tf_op jit(solution)/shard_map/all_gather | solution.py:31
  7.3 143.7 %all-gather.5.cloned.1.call-start = ((), (), s32[]{:S(2)}) async-start(), calls=%async_computation.3 | async-start | bytes 17301504 | tf_op jit(solution)/shard_map/all_gather | solution.py:34
  150.9 57.1 %copy-start.1 = (s32[32]{0:T(128)S(1)}, s32[32]{0:T(128)}, u32[]{:S(2)}) copy-start(s32[32]{0:T(128)} %param.7) | copy-start | bytes 388
  225.9 6.9 %copy-start = (f32[2048]{0:T(1024)S(1)}, f32[2048]{0:T(1024)}, u32[]{:S(2)}) copy-start(f32[2048]{0:T(1024)} %param.9) | copy-start | bytes 24580
  225.9 7.7 %copy-start.2 = (f32[8]{0:T(128)S(1)}, f32[8]{0:T(128)}, u32[]{:S(2)}) copy-start(f32[8]{0:T(128)} %param.8) | copy-start | bytes 100
  225.9 103.7 %all-to-all-start.1 = ((f32[1,8,64,2048]{3,2,0,1:T(8,128)}), f32[1,8,64,2048]{3,2,0,1:T(8,128)}, u32[]{:S(2)}, u32[]{:S(2)}) async-start(f32[1,8,64,2048]{3,2,0,1:T(8,128)} %bitcast.35), calls=%async_computation.1 | async-start | bytes 8388608 | tf_op jit(solution)/shard_map/all_to_all | solution.py:47
Sparse Core Ops, SparseCore 0:
  9.1 62.3 all-gather.2
  74.1 76.7 all-gather.4
where the time goes:
time: 343 us
  waiting for transfers between devices  212 us (62%)
  matrix products  67.2 us (20%)
  blocking collectives  26.2 us (8%)
  between operations  13.4 us (4%)
  local copies, waits for them, and re-layouts  10 us (3%)
  starting transfers between devices  6.91 us (2%)
  other arithmetic  6.76 us (2%)
    all_to_all x1, waiting for transfers between devices, body(): lax.all_to_all(direct, 'virt', split_axis=1, concat_axis=1, tiled=True)  94.8 us
    all_gather x1, waiting for transfers between devices, body(): lax.all_gather(own_rows, 'pair', axis=1, tiled=True)  79.3 us
    dot_general x1, matrix products, body(): jnp.einsum('xac,jbc->xjba', lax.all_gather(own_rows, 'pair', axis=1, tile...  57.1 us
    all_gather x1, waiting for transfers between devices, body(): int_full = lax.all_gather(ints, 'virt', axis=2, tiled=True)  37.2 us
    all_to_all x1, blocking collectives, body(): lax.all_to_all(amps, 'virt', split_axis=0, concat_axis=2, tiled=True)  26.2 us
    dot_general x1, matrix products, body(): jnp.einsum('xjbqp,qn->xjbnp', grouped, placing, precision=lax.Precision.H...  10.1 us
    reshape x1, local copies, waits for them, and re-layouts, body(): direct = jnp.einsum('xjbqp,qn->xjbnp', grouped, placing, precision=lax.Pr...  7.81 us
    all_to_all x1, starting transfers between devices, body(): lax.all_to_all(direct, 'virt', split_axis=1, concat_axis=1, tiled=True)  6.87 us
  transfers between devices with their start and end apart: 3, of which 3 were waited for; matrix products, arithmetic and copies ran while one was open for 1% of the time, Pallas kernels for 0%

commit v1 on v0

--- a/solution.py
+++ b/solution.py
@@ -28,7 +28,12 @@
         - e_vir[None, None, None, :]
     )
     own_rows = lax.all_to_all(amps, "virt", split_axis=0, concat_axis=2, tiled=True)
-    int_full = lax.all_gather(ints, "virt", axis=2, tiled=True)
+    ring = [ints]
+    for hop in range(7):
+        ring.append(lax.ppermute(ring[-1], "virt", [(dev, (dev + 1) % 8) for dev in range(8)]))
+    int_full = jnp.roll(
+        jnp.concatenate(ring[::-1], axis=2), (lax.axis_index("virt") + 1) * ring[0].shape[2], axis=2
+    )
     product = jnp.einsum(
         "xac,jbc->xjba",
         lax.all_gather(own_rows, "pair", axis=1, tiled=True),

time: 343 us -> 310 us (0.904)
  the two profiles are of different devices: /device:TPU:1 before, /device:TPU:20 now
where the time goes in v1:
time: 310 us
  waiting for transfers between devices  173 us (56%)
  matrix products  67.2 us (22%)
  blocking collectives  26.1 us (8%)
  local copies, waits for them, and re-layouts  17.7 us (6%)
  between operations  13.6 us (4%)
  other arithmetic  6.87 us (2%)
  starting transfers between devices  5.21 us (2%)
    ppermute x7, waiting for transfers between devices, body(): lax.ppermute(ring[-1], 'virt', [(dev, (dev + 1) % 8) for dev in range(8)])  87.7 us
    all_to_all x1, waiting for transfers between devices, body(): lax.all_to_all(direct, 'virt', split_axis=1, concat_axis=1, tiled=True)  85.3 us
    dot_general x1, matrix products, body(): jnp.einsum('xac,jbc->xjba', lax.all_gather(own_rows, 'pair', axis=1, tile...  57.1 us
    all_to_all x1, blocking collectives, body(): lax.all_to_all(amps, 'virt', split_axis=0, concat_axis=2, tiled=True)  26.1 us
    dot_general x1, matrix products, body(): jnp.einsum('xjbqp,qn->xjbnp', grouped, placing, precision=lax.Precision.H...  10.1 us
    reshape x1, local copies, waits for them, and re-layouts, body(): direct = jnp.einsum('xjbqp,qn->xjbnp', grouped, placing, precision=lax.Pr...  7.83 us
  transfers between devices with their start and end apart: 9, of which 8 were waited for; matrix products, arithmetic and copies ran while one was open for 3% of the time, Pallas kernels for 0%

profile of v1, /device:TPU:20, one launch (start us, length us, event | category | flops | bytes accessed | tf_op | source)
XLA Modules:
  0.0 309.7 jit_solution(5499904071191031908)
XLA Ops:
  6.5 26.1 %all_to_all.23 = f32[8,64,256]{2,1,0:T(8,128)S(1)} all-to-all(f32[8,64,256]{2,1,0:T(8,128)} %param.5), channel_id=1, replica_groups=mesh['pair'=32,'virt'=8] {'virt'}, dimensions={0} | all-to-all | bytes 1048576 | tf_op jit(solution)/shard_map/all_to_all | solution.py:30
  32.6 0.8 copy.14
  33.5 0.6 collective-permute-start
  34.1 12.7 %collective-permute-done = f32[8,64,256]{2,1,0:T(8,128)S(1)} collective-permute-done((f32[8,64,256]{2,1,0:T(8,128)}, f32[8,64,256]{2,1,0:T(8,128)S(1)}, u32[]{:S(2)}, u32[]{:S(2)}) %collective-permute-start) | collective-permute-done | bytes 524320 | tf_op jit(solution)/shard_map/ppermute | solution.py:33
  46.9 12.2 %collective-permute-done.1 = f32[8,64,256]{2,1,0:T(8,128)S(1)} collective-permute-done((f32[8,64,256]{2,1,0:T(8,128)S(1)}, f32[8,64,256]{2,1,0:T(8,128)S(1)}, u32[]{:S(2)}, u32[]{:S(2)}) %collective-permute-start.1) | collective-permute-done | bytes 524320 | tf_op jit(solution)/shard_map/ppermute | solution.py:33
  59.0 12.1 %collective-permute-done.2 = f32[8,64,256]{2,1,0:T(8,128)S(1)} collective-permute-done((f32[8,64,256]{2,1,0:T(8,128)S(1)}, f32[8,64,256]{2,1,0:T(8,128)S(1)}, u32[]{:S(2)}, u32[]{:S(2)}) %collective-permute-start.2) | collective-permute-done | bytes 524320 | tf_op jit(solution)/shard_map/ppermute | solution.py:33
  71.1 12.3 %collective-permute-done.3 = f32[8,64,256]{2,1,0:T(8,128)S(1)} collective-permute-done((f32[8,64,256]{2,1,0:T(8,128)S(1)}, f32[8,64,256]{2,1,0:T(8,128)S(1)}, u32[]{:S(2)}, u32[]{:S(2)}) %collective-permute-start.3) | collective-permute-done | bytes 524320 | tf_op jit(solution)/shard_map/ppermute | solution.py:33
  83.4 13.4 %collective-permute-done.4 = f32[8,64,256]{2,1,0:T(8,128)S(1)} collective-permute-done((f32[8,64,256]{2,1,0:T(8,128)S(1)}, f32[8,64,256]{2,1,0:T(8,128)S(1)}, u32[]{:S(2)}, u32[]{:S(2)}) %collective-permute-start.4) | collective-permute-done | bytes 524320 | tf_op jit(solution)/shard_map/ppermute | solution.py:33
  96.8 14.3 %collective-permute-done.5 = f32[8,64,256]{2,1,0:T(8,128)} collective-permute-done((f32[8,64,256]{2,1,0:T(8,128)S(1)}, f32[8,64,256]{2,1,0:T(8,128)}, u32[]{:S(2)}, u32[]{:S(2)}) %collective-permute-start.5) | collective-permute-done | bytes 524320 | tf_op jit(solution)/shard_map/ppermute | solution.py:33
  111.1 10.7 %collective-permute-done.6 = f32[8,64,256]{2,1,0:T(8,128)} collective-permute-done((f32[8,64,256]{2,1,0:T(8,128)}, f32[8,64,256]{2,1,0:T(8,128)}, u32[]{:S(2)}, u32[]{:S(2)}) %collective-permute-start.6) | collective-permute-done | bytes 524320 | tf_op jit(solution)/shard_map/ppermute | solution.py:33
  121.8 1.1 constant_dynamic-update-slice_fusion.15
  122.9 1.1 constant_dynamic-update-slice_fusion.14
  124.1 0.1 constant_dynamic-update-slice_fusion.13
  124.1 0.1 constant_dynamic-update-slice_fusion.12
  124.4 0.1 constant_dynamic-update-slice_fusion.9
  124.5 1.1 constant_dynamic-update-slice_fusion.7
  125.6 1.1 constant_dynamic-update-slice_fusion.6
  126.8 0.1 constant_dynamic-update-slice_fusion.5
  126.8 0.1 constant_dynamic-update-slice_fusion.4
  126.9 0.1 constant_dynamic-update-slice_fusion.3
  127.1 0.1 constant_dynamic-update-slice_fusion.1
  127.2 2.3 fusion.17
  129.5 57.1 %fusion.2 = f32[8,64,32,64]{3,1,2,0:T(8,128)S(1)} fusion(f32[32,64,2048,1]{2,1,0,3:T(8,128)} %bitcast.43, f32[8,64,2048,1]{2,1,3,0:T(8,128)} %fusion.17), kind=kOutput, calls=%fused_computation.3 | convolution fusion | flops 25769803776 | bytes 25165824 | tf_op jit(solution)/shard_map/xac,jbc->xjba/dot_general | solution.py:37
  186.7 10.1 %fusion.5 = f32[1,8,64,32,64]{4,3,2,1,0:T(8,128)} fusion(f32[8,64,32,64]{3,1,2,0:T(8,128)S(1)} %fusion.2, s32[32]{0:T(128)S(1)} %copy-done.2), kind=kOutput, calls=%fused_computation.7 | convolution fusion | flops 402654208 | bytes 8388736 | tf_op jit(solution)/shard_map/xjbqp,qn->xjbnp/dot_general | solution.py:45
  196.8 7.8 %reshape.79 = f32[1,8,64,2048]{3,2,1,0:T(8,128)} reshape(f32[1,8,64,32,64]{4,3,2,1,0:T(8,128)} %fusion.5) | data formatting | bytes 8388608 | tf_op jit(solution)/shard_map/reshape | solution.py:51
  204.6 4.5 %all-to-all-start.1 = ((f32[1,8,64,2048]{3,2,0,1:T(8,128)}), f32[1,8,64,2048]{3,2,0,1:T(8,128)}, u32[]{:S(2)}, u32[]{:S(2)}) async-start(f32[1,8,64,2048]{3,2,0,1:T(8,128)} %bitcast.40), calls=%async_computation.1 | async-start | bytes 8388608 | tf_op jit(solution)/shard_map/all_to_all | solution.py:52
  209.2 0.7 dynamic-slice.2
  209.9 0.8 gather_fusion
  210.6 0.7 broadcast_add_fusion
  211.3 0.1 broadcast_subtract_fusion
  211.4 85.3 %all-to-all-done.1 = f32[1,8,64,2048]{3,2,0,1:T(8,128)} async-done(((f32[1,8,64,2048]{3,2,0,1:T(8,128)}), f32[1,8,64,2048]{3,2,0,1:T(8,128)}, u32[]{:S(2)}, u32[]{:S(2)}) %all-to-all-start.1) | async-done | bytes 4194336 | tf_op jit(solution)/shard_map/all_to_all | solution.py:52
  296.7 6.1 %divide_bitcast_fusion = f32[1,8,64,2048]{3,2,1,0:T(8,128)} fusion(f32[1,8,64,2048]{3,2,0,1:T(8,128)} %all-to-all-done.1, f32[2048]{0:T(1024)S(1)} %copy-done, f32[8,64]{1,0:T(8,128)S(1)} %broadcast_subtract_fusion, f32[1,8,64,2048]{3,2,1,0:T(8,128)} %reshape.79), kind=kLoop, calls=%fused_computation.5 | loop fusion | flops 3145728 | bytes 12593152 | tf_op jit(solution)/shard_map/div | solution.py:53
  (24 shorter events, 0.4 us)
Async XLA Ops:
  6.5 117.9 %copy-start.1 = (f32[8,64,256]{2,1,0:T(8,128)S(1)}, f32[8,64,256]{2,1,0:T(8,128)}, u32[]{:S(2)}) copy-start(f32[8,64,256]{2,1,0:T(8,128)} %param.6) | copy-start | bytes 1572868
  6.5 123.0 %all-gather.2.cloned.1.call-start = ((), (), s32[]{:S(2)}) async-start(), calls=%async_computation.2 | async-start | bytes 17301504 | tf_op jit(solution)/shard_map/all_gather | solution.py:39
  33.5 13.4 %collective-permute-start = (f32[8,64,256]{2,1,0:T(8,128)}, f32[8,64,256]{2,1,0:T(8,128)S(1)}, u32[]{:S(2)}, u32[]{:S(2)}) collective-permute-start(f32[8,64,256]{2,1,0:T(8,128)} %param.6), channel_id=1, source_target_pairs={{0,1},{1,2},{2,3},{3,4},{4,5},{5,6},{6,7},{7,0},{8,9},{9,10},{10,1... | collective-permute-start | bytes 1572872 | tf_op jit(solution)/shard_map/ppermute | solution.py:33
  46.9 12.2 %collective-permute-start.1 = (f32[8,64,256]{2,1,0:T(8,128)S(1)}, f32[8,64,256]{2,1,0:T(8,128)S(1)}, u32[]{:S(2)}, u32[]{:S(2)}) collective-permute-start(f32[8,64,256]{2,1,0:T(8,128)S(1)} %collective-permute-done), channel_id=1, source_target_pairs={{0,1},{1,2},{2,3},{3,4},{4,5},{5,6},{6,7},{7,0},{8,9},{9,10},{10,1... | collective-permute-start | bytes 1572872 | tf_op jit(solution)/shard_map/ppermute | solution.py:33
  59.0 12.1 %collective-permute-start.2 = (f32[8,64,256]{2,1,0:T(8,128)S(1)}, f32[8,64,256]{2,1,0:T(8,128)S(1)}, u32[]{:S(2)}, u32[]{:S(2)}) collective-permute-start(f32[8,64,256]{2,1,0:T(8,128)S(1)} %collective-permute-done.1), channel_id=1, source_target_pairs={{0,1},{1,2},{2,3},{3,4},{4,5},{5,6},{6,7},{7,0},{8,9},{9,10},{10,1... | collective-permute-start | bytes 1572872 | tf_op jit(solution)/shard_map/ppermute | solution.py:33
  71.1 12.3 %collective-permute-start.3 = (f32[8,64,256]{2,1,0:T(8,128)S(1)}, f32[8,64,256]{2,1,0:T(8,128)S(1)}, u32[]{:S(2)}, u32[]{:S(2)}) collective-permute-start(f32[8,64,256]{2,1,0:T(8,128)S(1)} %collective-permute-done.2), channel_id=1, source_target_pairs={{0,1},{1,2},{2,3},{3,4},{4,5},{5,6},{6,7},{7,0},{8,9},{9,10},{10,1... | collective-permute-start | bytes 1572872 | tf_op jit(solution)/shard_map/ppermute | solution.py:33
  83.4 13.4 %collective-permute-start.4 = (f32[8,64,256]{2,1,0:T(8,128)S(1)}, f32[8,64,256]{2,1,0:T(8,128)S(1)}, u32[]{:S(2)}, u32[]{:S(2)}) collective-permute-start(f32[8,64,256]{2,1,0:T(8,128)S(1)} %collective-permute-done.3), channel_id=1, source_target_pairs={{0,1},{1,2},{2,3},{3,4},{4,5},{5,6},{6,7},{7,0},{8,9},{9,10},{10,1... | collective-permute-start | bytes 1572872 | tf_op jit(solution)/shard_map/ppermute | solution.py:33
  96.8 14.3 %collective-permute-start.5 = (f32[8,64,256]{2,1,0:T(8,128)S(1)}, f32[8,64,256]{2,1,0:T(8,128)}, u32[]{:S(2)}, u32[]{:S(2)}) collective-permute-start(f32[8,64,256]{2,1,0:T(8,128)S(1)} %collective-permute-done.4), channel_id=1, source_target_pairs={{0,1},{1,2},{2,3},{3,4},{4,5},{5,6},{6,7},{7,0},{8,9},{9,10},{10,1... | collective-permute-start | bytes 1572872 | tf_op jit(solution)/shard_map/ppermute | solution.py:33
  111.1 10.7 %collective-permute-start.6 = (f32[8,64,256]{2,1,0:T(8,128)}, f32[8,64,256]{2,1,0:T(8,128)}, u32[]{:S(2)}, u32[]{:S(2)}) collective-permute-start(f32[8,64,256]{2,1,0:T(8,128)} %collective-permute-done.5), channel_id=1, source_target_pairs={{0,1},{1,2},{2,3},{3,4},{4,5},{5,6},{6,7},{7,0},{8,9},{9,10},{10,1... | collective-permute-start | bytes 1572872 | tf_op jit(solution)/shard_map/ppermute | solution.py:33
  129.5 57.2 %copy-start.2 = (s32[32]{0:T(128)S(1)}, s32[32]{0:T(128)}, u32[]{:S(2)}) copy-start(s32[32]{0:T(128)} %param.7) | copy-start | bytes 388
  196.8 12.4 %copy-start.3 = (f32[8]{0:T(128)S(1)}, f32[8]{0:T(128)}, u32[]{:S(2)}) copy-start(f32[8]{0:T(128)} %param.8) | copy-start | bytes 100
  196.8 13.1 %copy-start = (f32[2048]{0:T(1024)S(1)}, f32[2048]{0:T(1024)}, u32[]{:S(2)}) copy-start(f32[2048]{0:T(1024)} %param.9) | copy-start | bytes 24580
  204.6 92.1 %all-to-all-start.1 = ((f32[1,8,64,2048]{3,2,0,1:T(8,128)}), f32[1,8,64,2048]{3,2,0,1:T(8,128)}, u32[]{:S(2)}, u32[]{:S(2)}) async-start(f32[1,8,64,2048]{3,2,0,1:T(8,128)} %bitcast.40), calls=%async_computation.1 | async-start | bytes 8388608 | tf_op jit(solution)/shard_map/all_to_all | solution.py:52
Sparse Core Ops, SparseCore 0:
  33.6 71.8 all-gather.1
